TPU v7x, 32 devices: a whole 2x2x4 slice. The times are simulated.
32 devices in a mesh: parts: 2 (over y), tm: 4 (over z), axial: 2 (over x), chan: 2 (over core).
Axes of the slice: x: 2, y: 2, z: 4, core: 2. Of those that a mesh axis runs over, the one named last changes fastest.
Arguments:
- frames_in: bfloat16 [48, 8, 64, 128], P(('parts', 'tm'), 'axial'), parts along dimension 0, may hold values from -6 to 6
- spatial_weight: bfloat16 [6, 3, 64, 144], P('parts', None, None, 'chan'), parts along dimension 0, may hold values from -0.25 to 0.25
- temporal_weight: bfloat16 [6, 144, 64], P('parts', 'chan'), parts along dimension 0, may hold values from -0.3125 to 0.3125
- upstream: bfloat16 [48, 8, 64, 128], P(('parts', 'tm'), 'axial'), parts along dimension 0, may hold values from -6 to 6
Outputs:
- output: bfloat16 [48, 8, 64, 128], P(('parts', 'tm'), 'axial', 'chan'), parts along dimension 0
- input_grad: bfloat16 [48, 8, 64, 128], P(('parts', 'tm'), 'axial', 'chan'), parts along dimension 0
- spatial_grad: float32 [6, 3, 64, 144], P('parts', None, None, 'chan'), parts along dimension 0
- temporal_grad: float32 [6, 144, 64], P('parts', 'chan'), parts along dimension 0
There are 2 independent parts, one for each index of `parts`. A program takes and returns all parts, laid end to end along the dimension named above; each array names one. Nothing has to cross between parts.
All inputs are finite; a program needn't handle non-finite values.
Results may differ from a plain program's by a relative error of at most 0.009.
Values may be sent and summed in bfloat16 or wider, within the bound.
No kernel may reach another device: no remote copies, remote signals or barrier semaphores. Data moves between devices by JAX's collectives and lax.ppermute only.
A program may use at most 64 MiB of HBM per device.

v0:
```python
import functools
import math

import jax
import jax.numpy as jnp
from jax import lax
from jax.experimental import pallas as pl
from jax.experimental.pallas import tpu as pltpu
from jax.sharding import PartitionSpec as P

F32 = jnp.float32
BF16 = jnp.bfloat16
LANES = 128
HBM = pl.BlockSpec(memory_space=pltpu.HBM)
VMEM = pl.BlockSpec(memory_space=pltpu.VMEM)


def ring(count, step):
    return [(i, (i + step) % count) for i in range(count)]


def pairs(count, stride):
    return [(i, i ^ stride) for i in range(count)]


def facing(count):
    order = []
    for i in range(count):
        order += [(2 * i, 2 * ((i - 1) % count) + 1), (2 * i + 1, 2 * ((i + 1) % count))]
    return order


def dot(a, b):
    return jnp.dot(a, b, preferred_element_type=F32)


def dot_nt(a, b):
    return lax.dot_general(a, b, (((1,), (1,)), ((), ())), preferred_element_type=F32)


def moved(value, step):
    width = value.shape[1]
    column = lax.broadcasted_iota(jnp.int32, value.shape, 1)
    edge = 0 if step > 0 else width - 1
    return jnp.where(column == edge, 0.0, pltpu.roll(value, step % width, 1))


def pieces(depth, total):
    blocks, row = [], 0
    for first in range(0, total - total % LANES, LANES):
        blocks.append((row, 0, 0, first, depth, LANES))
        row += depth
    rest = total % LANES
    if rest:
        fold = LANES // rest
        if LANES % rest or depth % (8 * fold):
            fold = 1
        part = depth // fold
        for g in range(fold):
            blocks.append((row, g * rest, g * part, total - rest, part, rest))
        row += part
    return blocks, row


def half_rows(depth, total):
    return -(-pieces(depth, total)[1] // 32) * 16


def stage_kernel(split, x, u, edge, frame, sems):
    frames, rows = x.shape[:2]
    core = lax.axis_index("chan")
    if split:
        row = jnp.where(lax.axis_index("axial") == 0, rows - 1, 0)
        picked = pl.ds(core * (frames // 2), frames // 2)
    else:
        row = core * (rows - 1)
        picked = pl.ds(0, frames)
    copies = [
        pltpu.make_async_copy(u.at[core * (frames - 1)], frame, sems.at[0]),
        pltpu.make_async_copy(x.at[picked, row], edge, sems.at[1]),
    ]
    for copy in copies:
        copy.start()
    for copy in copies:
        copy.wait()


def prepare(sw, tw, wf, twf):
    channels, mid = tw.shape[1:]
    for j in range(3):
        wf[j * mid : (j + 1) * mid] = sw[:, j].reshape(3 * channels, mid).astype(F32).T
    twf[...] = jnp.concatenate([tw[k].astype(F32) for k in (2, 1, 0)], 0).T
    return wf[...].astype(BF16), twf[...].astype(BF16)


def activations(w_taps, w_act, field, cot, width):
    mid = w_act.shape[0]
    taps = dot(w_taps, field)
    act = dot(w_act, cot)
    hids, grads = [], []
    for first in range(0, field.shape[1], width):
        cols = slice(first, first + width)
        pre = taps[mid : 2 * mid, cols] + moved(taps[:mid, cols], 1) + moved(taps[2 * mid :, cols], -1)
        s = 0.5 * jnp.tanh(0.5 * pre) + 0.5
        hids.append(pre * s)
        grads.append(act[:, cols] * s * (1.0 + pre * (1.0 - s)))
    return hids, grads


def gathered(xp, up, h, picked):
    depth = 3 * xp.shape[2]
    width = xp.shape[3]
    field = jnp.concatenate([xp[f, pl.ds(h, 3)].reshape(depth, width) for f in picked], 1)
    cot = jnp.concatenate([jnp.concatenate([up[f + d, h] for d in range(3)], 0) for f in picked], 1)
    return field, cot


def inner_rows(axial_count, rows):
    if axial_count == 2:
        low = lax.axis_index("axial") == 0
        return jnp.where(low, 0, 1), rows - 1, [jnp.where(low, rows - 1, 0)]
    return 1, rows - 2, [0, rows - 1]


def cell_grads(xp, up, w_taps, w_act, groups, store):
    fields, cots, shifts, owns = [], [], [], []
    width = xp.shape[3]
    for h, picked in groups:
        field, cot = gathered(xp, up, h, picked)
        hids, grads = activations(w_taps, w_act, field, cot, width)
        shifts.append(
            jnp.concatenate(
                [
                    jnp.concatenate([moved(v, -1) for v in grads], 1),
                    jnp.concatenate(grads, 1),
                    jnp.concatenate([moved(v, 1) for v in grads], 1),
                ],
                0,
            ).astype(BF16)
        )
        hids = [v.astype(BF16) for v in hids]
        owns.append(jnp.concatenate(hids, 1))
        for f, hid, grad in zip(picked, hids, grads):
            store(h, f, hid, grad.astype(BF16))
        fields.append(field)
        cots.append(cot)
    return (
        dot_nt(jnp.concatenate(fields, 1), jnp.concatenate(shifts, 1)),
        dot_nt(jnp.concatenate(cots, 1), jnp.concatenate(owns, 1)),
    )


def inner_kernel(dims, *refs):
    frames, rows, channels, width, mid, own_c, rank_count, axial_count, group = dims
    x, u, sw, tw = refs[:4]
    hid_out, grad_out, acc_out, xp, up, taps_out, act_out, wf, twf = refs[4:]
    for f in range(frames):
        for at in (0, rows + 1):
            xp[f, at] = jnp.zeros((channels, width), BF16)
        for h in range(rows):
            xp[f, h + 1] = x[f, h]
            up[f + 1, h] = u[f, h]
    for at in (0, frames + 1):
        up[at] = jnp.zeros(up.shape[1:], BF16)
    w_taps, w_act = prepare(sw, tw, wf, twf)
    taps_out[...] = w_taps
    act_out[...] = w_act

    first, count, _ = inner_rows(axial_count, rows)

    def store(h, f, hid, grad):
        hid_out[h - first, f - 1] = hid
        grad_out[h - first, f - 1] = grad

    groups = [(first + i, (f, f + 1)) for i in range(count) for f in range(1, frames - 1, 2)]
    w_part, t_part = cell_grads(xp, up, w_taps, w_act, groups, store)
    acc_out[:, : 3 * mid] = w_part
    acc_out[:, 3 * mid :] = t_part


def grads_kernel(dims, *refs):
    frames, rows, channels, width, mid, own_c, rank_count, axial_count, group = dims
    hid_in, grad_in, acc_in, x, u, edge, frame, swapped, taps_in, act_in = refs[:10]
    hid_out, grad_out, xp, up, keep, send, edges, acc, packed = refs[10:]
    axial = lax.axis_index("axial")
    core = lax.axis_index("chan")
    w_taps, w_act = taps_in[...], act_in[...]

    has_lo = (axial > 0).astype(BF16)
    has_hi = (axial < axial_count - 1).astype(BF16)
    part = edge.shape[0]
    edges[pl.ds(core * part, part)] = edge[...]
    edges[pl.ds((1 - core) * part, part)] = swapped[0:part]
    at_hi = 2 * part - frames
    for f in range(frames):
        xp[f, 0] = edges[f] * has_lo
        xp[f, rows + 1] = edges[at_hi + f] * has_hi
        for h in range(rows):
            xp[f, h + 1] = x[f, h + 1]
            up[f + 1, h] = u[f + 1, h]
    up[core * (frames + 1)] = frame[...]
    up[(1 - core) * (frames + 1)] = swapped[part:]

    first, count, others = inner_rows(axial_count, rows)

    def store(h, f, hid, grad):
        hid_out[h, f] = hid
        grad_out[h, f] = grad

    for i in range(count):
        for f in range(1, frames - 1):
            store(first + i, f, hid_in[i, f - 1], grad_in[i, f - 1])
    groups = [(first + i, (0, frames - 1)) for i in range(count)]
    groups += [(h, (f, f + 1)) for h in others for f in range(0, frames, 2)]
    w_part, t_part = cell_grads(xp, up, w_taps, w_act, groups, store)
    factor = 1.0 / math.sqrt(frames * rows * width * rank_count)
    acc[:, : 3 * mid] = (acc_in[:, : 3 * mid] + w_part) * factor
    acc[:, 3 * mid :] = (acc_in[:, 3 * mid :] + t_part) * factor

    blocks, used = pieces(*acc.shape)
    size = packed.shape[0] // 2
    packed[used:] = jnp.zeros((2 * size - used, LANES), F32)
    for at, lane, source, column, depth, total in blocks:
        packed[at : at + depth, lane : lane + total] = acc[source : source + depth, column : column + total]
    mine = lax.rem(axial, 2)
    keep[...] = packed[pl.ds(pl.multiple_of(mine * size, 16), size)]
    send[...] = packed[pl.ds(pl.multiple_of((1 - mine) * size, 16), size)].astype(send.dtype)


def fields_kernel(dims, *refs):
    frames, rows, channels, width, mid, own_c, rank_count, axial_count, group = dims
    hid_in, grad_in, xp, up, sw, tw, sw_other, tw_other = refs[:8]
    out, out_lo, out_hi, ig, ig_lo, ig_hi, wf, twf, twt, wg, ig_acc = refs[8:]
    core = lax.axis_index("chan")
    first_c = pl.multiple_of(core * own_c, own_c)
    own = pl.ds(first_c, own_c)
    w_taps, w_act = prepare(sw_other, tw_other, wf, twf)
    for k in range(3):
        twt[k * own_c : (k + 1) * own_c] = jnp.concatenate(
            [w[k, own].astype(F32) for w in (tw, tw_other)], 1
        ).astype(BF16)
    for i in range(3):
        for j in range(3):
            at = (i * 3 + j) * own_c
            wg[at : at + own_c] = jnp.concatenate([w[i, j, own].astype(F32) for w in (sw, sw_other)], 1).astype(BF16)
    ig_acc[...] = jnp.zeros_like(ig_acc)

    def row(h, carry):
        out_terms = {}
        for first in range(0, frames, group):
            field, cot = gathered(xp, up, h, range(first, first + group))
            hids, grads = activations(w_taps, w_act, field, cot, width)
            picked = range(first, first + group)
            hid = [jnp.concatenate([hid_in[h, f].astype(F32), v], 0) for f, v in zip(picked, hids)]
            grad = [jnp.concatenate([grad_in[h, f].astype(F32), v], 0) for f, v in zip(picked, grads)]
            y_out = dot(twt[...], jnp.concatenate(hid, 1).astype(BF16))
            y_in = dot(wg[...], jnp.concatenate(grad, 1).astype(BF16))
            for g in range(group):
                f = first + g
                cols = slice(g * width, (g + 1) * width)
                for k in range(3):
                    out_terms.setdefault(f - k + 1, []).append(y_out[k * own_c : (k + 1) * own_c, cols])
                for i in range(3):
                    at = i * 3 * own_c
                    ig_acc[f, h + i] += (
                        y_in[at + own_c : at + 2 * own_c, cols]
                        + moved(y_in[at : at + own_c, cols], -1)
                        + moved(y_in[at + 2 * own_c : at + 3 * own_c, cols], 1)
                    )
        for f, terms in out_terms.items():
            total = functools.reduce(lambda a, b: a + b, terms)
            if f < 0:
                out_lo[0, h] = total.astype(BF16)
            elif f >= frames:
                out_hi[0, h] = total.astype(BF16)
            else:
                out[f, h] = total
        return carry

    lax.fori_loop(0, rows, row, 0)
    for f in range(frames):
        ig_lo[f] = ig_acc[f, 0].astype(BF16)
        ig_hi[f] = ig_acc[f, rows + 1].astype(BF16)
        for h in range(rows):
            ig[f, h] = ig_acc[f, h + 1]


def outputs_kernel(axial_count, own, from_lo, from_hi, ig_own, ig_from_lo, ig_from_hi, out, ig):
    frames, rows = own.shape[:2]
    axial = lax.axis_index("axial")
    has_lo = (axial > 0).astype(F32)
    has_hi = (axial < axial_count - 1).astype(F32)
    for f in range(frames):
        for h in range(rows):
            total = own[f, h]
            if f == 0:
                total = total + from_lo[0, h].astype(F32)
            if f == frames - 1:
                total = total + from_hi[0, h].astype(F32)
            out[f, h] = total.astype(BF16)
            total = ig_own[f, h]
            if h == 0:
                total = total + ig_from_lo[f].astype(F32) * has_lo
            if h == rows - 1:
                total = total + ig_from_hi[f].astype(F32) * has_hi
            ig[f, h] = total.astype(BF16)


def unpack_kernel(mine, other, sg, tg, packed, acc):
    channels, mid = tg.shape[1:]
    size = mine.shape[0]
    half = lax.rem(lax.axis_index("axial"), 2)
    packed[pl.ds(pl.multiple_of(half * size, 16), size)] = mine[...].astype(F32)
    packed[pl.ds(pl.multiple_of((1 - half) * size, 16), size)] = other[...].astype(F32)
    for at, lane, source, column, depth, total in pieces(*acc.shape)[0]:
        acc[source : source + depth, column : column + total] = packed[at : at + depth, lane : lane + total]
    for i in range(3):
        rows = slice(i * channels, (i + 1) * channels)
        for j in range(3):
            sg[i, j] = acc[rows, j * mid : (j + 1) * mid]
        tg[2 - i] = acc[rows, 3 * mid :]


def call(kernel, name, out_shape, count, limit, scratch=(), in_specs=None, flops=0):
    return pl.pallas_call(
        kernel,
        out_shape=out_shape,
        in_specs=in_specs or [VMEM] * count,
        out_specs=[VMEM] * len(out_shape),
        scratch_shapes=list(scratch),
        compiler_params=pltpu.CompilerParams(vmem_limit_bytes=int(limit * 1024 * 1024)),
        cost_estimate=pl.CostEstimate(flops=flops, bytes_accessed=1 << 20, transcendentals=0) if flops else None,
        name=name,
    )


def shards(frames_in, spatial_weight, temporal_weight, upstream):
    frames, rows, channels, width = frames_in.shape
    mid = temporal_weight.shape[1]
    axial_count = lax.axis_size("axial")
    tm_count = lax.axis_size("tm")
    core_count = lax.axis_size("chan")
    rank_count = tm_count * axial_count
    axial = lax.axis_index("axial")
    own_c = channels // core_count
    group = 2 if frames % 2 == 0 else 1
    dims = (frames, rows, channels, width, mid, own_c, rank_count, axial_count, group)
    size = half_rows(3 * channels, 4 * mid)
    sds = jax.ShapeDtypeStruct

    split = axial_count == 2 and frames % 2 == 0
    edge_count = frames // 2 if split else frames
    turned = jnp.swapaxes(temporal_weight, 1, 2)
    edge, frame = call(
        functools.partial(stage_kernel, split),
        "stage",
        [sds((edge_count, channels, width), BF16), sds((rows, channels, width), BF16)],
        2,
        60,
        [pltpu.SemaphoreType.DMA((2,))],
        [HBM] * 2,
    )(frames_in, upstream)
    frame = lax.ppermute(frame, ("tm", "chan"), facing(tm_count))
    if split:
        edge = lax.ppermute(edge, "axial", ring(2, 1))
    else:
        edge = lax.ppermute(edge, ("axial", "chan"), facing(axial_count))
    sw_other = lax.ppermute(spatial_weight, "chan", ring(2, 1))
    tw_other = lax.ppermute(turned, "chan", ring(2, 1))

    own_shape = (frames, rows, own_c, width)
    inner = (inner_rows(axial_count, rows)[1], frames - 2, mid, width)
    cells = (rows, frames, mid, width)
    xp_shape = (frames, rows + 2, channels, width)
    up_shape = (frames + 2, rows, channels, width)
    total = (3 * channels, 4 * mid)
    hid, grad, acc, xp, up, w_taps, w_act = call(
        functools.partial(inner_kernel, dims),
        "inner_cells",
        [
            sds(inner, BF16),
            sds(inner, BF16),
            sds(total, F32),
            sds(xp_shape, BF16),
            sds(up_shape, BF16),
            sds((3 * mid, 3 * channels), BF16),
            sds((mid, 3 * channels), BF16),
        ],
        4,
        16,
        [pltpu.VMEM((3 * mid, 3 * channels), F32), pltpu.VMEM((mid, 3 * channels), F32)],
        flops=1 << 31,
    )(frames_in, upstream, spatial_weight, turned)
    edge, frame, acc = lax.optimization_barrier((edge, frame, acc))
    swapped = lax.ppermute(jnp.concatenate([edge, frame], 0), "chan", ring(2, 1))
    hid, grad, xp, up, keep, send = call(
        functools.partial(grads_kernel, dims),
        "weight_grads",
        [
            sds(cells, BF16),
            sds(cells, BF16),
            sds(xp_shape, BF16),
            sds(up_shape, BF16),
            sds((size, LANES), F32),
            sds((size, LANES), BF16 if axial_count == 2 else F32),
        ],
        10,
        16,
        [
            pltpu.VMEM((2 * edge_count, channels, width), BF16),
            pltpu.VMEM(total, F32),
            pltpu.VMEM((2 * size, LANES), F32),
        ],
    )(hid, grad, acc, xp, up, edge, frame, swapped, w_taps, w_act)

    got = lax.ppermute(send, "axial", ring(2, 1)) if axial_count == 2 else None

    out_own, out_lo, out_hi, ig_own, ig_lo, ig_hi = call(
        functools.partial(fields_kernel, dims),
        "field_products",
        [
            sds(own_shape, F32),
            sds((1, rows, own_c, width), BF16),
            sds((1, rows, own_c, width), BF16),
            sds(own_shape, F32),
            sds((frames, own_c, width), BF16),
            sds((frames, own_c, width), BF16),
        ],
        8,
        16,
        [
            pltpu.VMEM((3 * mid, 3 * channels), F32),
            pltpu.VMEM((mid, 3 * channels), F32),
            pltpu.VMEM((3 * own_c, 2 * mid), BF16),
            pltpu.VMEM((9 * own_c, 2 * mid), BF16),
            pltpu.VMEM((frames, rows + 2, own_c, width), F32),
        ],
        flops=1 << 31,
    )(hid, grad, xp, up, spatial_weight, turned, sw_other, tw_other)
    if got is not None:
        got, out_lo, out_hi, ig_lo, ig_hi = lax.optimization_barrier((got, out_lo, out_hi, ig_lo, ig_hi))

    from_hi = lax.ppermute(out_lo, "tm", ring(tm_count, -1))
    from_lo = lax.ppermute(out_hi, "tm", ring(tm_count, 1))
    if axial_count == 2:
        ig_from_lo = ig_from_hi = lax.ppermute(jnp.where(axial == 0, ig_hi, ig_lo), "axial", ring(2, 1))
    else:
        ig_from_hi = lax.ppermute(ig_lo, "axial", ring(axial_count, -1))
        ig_from_lo = lax.ppermute(ig_hi, "axial", ring(axial_count, 1))

    if axial_count == 2 and tm_count & (tm_count - 1) == 0:
        mine = lax.optimization_barrier((keep + got.astype(F32)).astype(BF16))
        stride = 1
        while stride < tm_count:
            mine = lax.optimization_barrier(mine + lax.ppermute(mine, "tm", pairs(tm_count, stride)))
            stride *= 2
        other = lax.ppermute(mine, "axial", ring(2, 1))
    else:
        odd = lax.rem(axial, 2) == 1
        low, high = jnp.where(odd, send, keep), jnp.where(odd, keep, send)
        low, high = lax.psum((low, high), ("tm", "axial"))
        mine, other = jnp.where(odd, high, low), jnp.where(odd, low, high)

    output, input_grad = call(
        functools.partial(outputs_kernel, axial_count),
        "outputs",
        [sds(own_shape, BF16), sds(own_shape, BF16)],
        6,
        4,
        flops=1 << 29,
    )(out_own, from_lo, from_hi, ig_own, ig_from_lo, ig_from_hi)
    spatial_grad, temporal_grad = call(
        unpack_kernel,
        "unpack",
        [sds((3, 3, channels, mid), F32), sds((3, channels, mid), F32)],
        2,
        4,
        [pltpu.VMEM((2 * size, LANES), F32), pltpu.VMEM((3 * channels, 4 * mid), F32)],
    )(mine, other)
    return output, input_grad, spatial_grad, jnp.swapaxes(temporal_grad, 1, 2)


def solution(mesh):
    placed = (
        P(("parts", "tm"), "axial", None, None),
        P("parts", None, None, "chan"),
        P("parts", "chan", None),
        P(("parts", "tm"), "axial", None, None),
    )
    return jax.shard_map(
        shards,
        mesh=mesh,
        in_specs=placed,
        out_specs=(
            P(("parts", "tm"), "axial", "chan", None),
            P(("parts", "tm"), "axial", "chan", None),
            P("parts", None, None, "chan"),
            P("parts", "chan", None),
        ),
        check_vma=False,
    )
```

profile of v0, /device:TPU:0, one launch (start us, length us, event | category | flops | bytes accessed | tf_op | source)
XLA Modules:
  0.0 35.8 jit_solution(6879951672215309669)
XLA Ops:
  0.6 0.0 copy-start
  0.6 0.0 copy-start.1
  0.7 1.6 %stage.1 = (bf16[3,64,128]{2,1,0:T(8,128)(2,1)}, bf16[4,64,128]{2,1,0:T(8,128)(2,1)}) custom-call(bf16[6,4,64,128]{3,2,1,0:T(8,128)(2,1)} %x.1, bf16[6,4,64,128]{3,2,1,0:T(8,128)(2,1)} %u.1), custom_call_target="tpu_custom_call" | custom-call | tf_op jit(solution)/shard_map/stage/pallas_call | solution.py:354
  2.2 4.6 %collective-permute-start.1 = (bf16[4,64,128]{2,1,0:T(8,128)(2,1)}, bf16[4,64,128]{2,1,0:T(8,128)(2,1)S(1)}, u32[]{:S(2)}, u32[]{:S(2)}) collective-permute-start(bf16[4,64,128]{2,1,0:T(8,128)(2,1)} %get-tuple-element.40), channel_id=1, source_target_pairs={{0,13},{1,4},{4,1},{5,8},{8,5},{9,12},{12,9},{13,0},{2,15},{3,6},{... | collective-permute-start | bytes 196616 | tf_op jit(solution)/shard_map/ppermute | solution.py:363
  6.8 1.5 %collective-permute-start = (bf16[3,64,128]{2,1,0:T(8,128)(2,1)}, bf16[3,64,128]{2,1,0:T(8,128)(2,1)S(1)}, u32[]{:S(2)}, u32[]{:S(2)}) collective-permute-start(bf16[3,64,128]{2,1,0:T(8,128)(2,1)} %get-tuple-element.39), channel_id=1, source_target_pairs={{0,2},{2,0},{1,3},{3,1},{4,6},{6,4},{5,7},{7,5},{8,10},{10,8},{9,1... | collective-permute-start | bytes 147464 | tf_op jit(solution)/shard_map/ppermute | solution.py:365
  8.3 0.0 copy-done
  8.3 0.0 copy-done.1
  8.3 0.0 copy-start.2
  8.3 0.9 %copy-done.2 = bf16[3,3,64,72]{3,2,1,0:T(8,128)(2,1)S(1)} copy-done((bf16[3,3,64,72]{3,2,1,0:T(8,128)(2,1)S(1)}, bf16[3,3,64,72]{3,2,1,0:T(8,128)(2,1)}, u32[]{:S(2)}) %copy-start.2) | copy-done | bytes 82968
  9.2 0.0 copy-start.3
  9.2 0.8 %copy-done.3 = bf16[3,72,64]{1,2,0:T(8,128)(2,1)S(1)} copy-done((bf16[3,72,64]{1,2,0:T(8,128)(2,1)S(1)}, bf16[3,72,64]{1,2,0:T(8,128)(2,1)}, u32[]{:S(2)}) %copy-start.3) | copy-done | bytes 27672
  10.0 1.3 %inner_cells.1 = (bf16[3,4,72,128]{3,2,1,0:T(8,128)(2,1)S(1)}, bf16[3,4,72,128]{3,2,1,0:T(8,128)(2,1)S(1)}, f32[192,288]{1,0:T(8,128)S(1)}, bf16[6,6,64,128]{3,2...) custom-call(bf16[6,4,64,128]{3,2,1,0:T(8,128)(2,1)S(1)} %copy-done, ...), custom_call_target="tpu_custom_call" | custom-call | flops 2147483648 | bytes 1048576 | tf_op jit(solution)/shard_map/inner_cells/pallas_call | solution.py:377
  11.3 0.0 collective-permute-done.refs_5_
  11.3 0.0 collective-permute-done.1.refs_6_
  11.3 0.1 collective-permute-start.2
  11.4 0.5 %collective-permute-start.3 = (bf16[3,3,64,72]{3,2,1,0:T(8,128)(2,1)S(1)}, bf16[3,3,64,72]{3,2,1,0:T(8,128)(2,1)S(1)}, u32[]{:S(2)}, u32[]{:S(2)}) collective-permute-start(bf16[3,3,64,72]{3,2,1,0:T(8,128)(2,1)S(1)} %copy-done.2), channel_id=1, source_target_pairs={{0,1},{1,0},{2,3},{3,2},{4,5},{5,4},{6,7},{7,6},{8,9},{9,8},{10,11... | collective-permute-start | bytes 248840 | tf_op jit(solution)/shard_map/ppermute | solution.py:368
  11.9 0.1 collective-permute-start.4
  12.0 0.7 %collective-permute-done.2.refs_7_ = bf16[7,64,128]{2,1,0:T(8,128)(2,1)S(1)} collective-permute-done((bf16[7,64,128]{2,1,0:T(8,128)(2,1)S(1)}, bf16[7,64,128]{2,1,0:T(8,128)(2,1)S(1)}, u32[]{:S(2)}, u32[]{:S(2)}) %collective-permute-start.2) | collective-permute-done | bytes 114720 | tf_op jit(solution)/shard_map/ppermute | solution.py:395
  12.7 1.3 %weight_grads.1 = (bf16[4,6,72,128]{3,2,1,0:T(8,128)(2,1)S(1)}, bf16[4,6,72,128]{3,2,1,0:T(8,128)(2,1)S(1)}, bf16[6,6,64,128]{3,2,1,0:T(8,128)(2,1)S(1)}, bf16[8...) custom-call(bf16[3,4,72,128]{3,2,1,0:T(8,128)(2,1)S(1)} %get-tuple-element.37.refs_0_, ...), custom_call_target="tpu_custom_call" | custom-call | tf_op jit(solution)/shard_map/weight_grads/pallas_call | solution.py:396
  14.0 1.4 %collective-permute-start.5 = (bf16[224,128]{1,0:T(8,128)(2,1)S(1)}, bf16[224,128]{1,0:T(8,128)(2,1)S(1)}, u32[]{:S(2)}, u32[]{:S(2)}) collective-permute-start(bf16[224,128]{1,0:T(8,128)(2,1)S(1)} %get-tuple-element.54), channel_id=1, source_target_pairs={{0,2},{2,0},{1,3},{3,1},{4,6},{6,4},{5,7},{7,5},{8,10},{10,8},{9,1... | collective-permute-start | bytes 172040 | tf_op jit(solution)/shard_map/ppermute | solution.py:416
  15.4 0.0 collective-permute-done.4.refs_7_
  15.4 0.0 collective-permute-done.3.refs_6_
  15.4 4.9 %field_products.1 = (f32[6,4,32,128]{3,2,1,0:T(8,128)S(1)}, bf16[1,4,32,128]{3,2,1,0:T(8,128)(2,1)S(1)}, bf16[1,4,32,128]{3,2,1,0:T(8,128)(2,1)S(1)}, f32[6,4,32...) custom-call(bf16[4,6,72,128]{3,2,1,0:T(8,128)(2,1)S(1)} %get-tuple-element.49.refs_0_, ...), custom_call_target="tpu_custom_call" | custom-call | flops 2147483648 | bytes 1048576 | tf_op jit(solution)/shard_map/field_products/pallas_call | solution.py:418
  20.4 0.0 collective-permute-done.5
  20.4 0.1 collective-permute-start.9
  20.5 4.2 %collective-permute-done.9 = bf16[224,128]{1,0:T(8,128)(2,1)S(1)} collective-permute-done((bf16[224,128]{1,0:T(8,128)(2,1)S(1)}, bf16[224,128]{1,0:T(8,128)(2,1)S(1)}, u32[]{:S(2)}, u32[]{:S(2)}) %collective-permute-start.9) | collective-permute-done | bytes 57376 | tf_op jit(solution)/shard_map/ppermute | solution.py:455
  24.7 0.1 collective-permute-start.10
  24.8 1.4 %collective-permute-start.8 = (bf16[6,32,128]{2,1,0:T(8,128)(2,1)S(1)}, bf16[6,32,128]{2,1,0:T(8,128)(2,1)S(1)}, u32[]{:S(2)}, u32[]{:S(2)}) collective-permute-start(bf16[6,32,128]{2,1,0:T(8,128)(2,1)S(1)} %broadcast_select_fusion), channel_id=1, source_target_pairs={{0,2},{2,0},{1,3},{3,1},{4,6},{6,4},{5,7},{7,5},{8,10},{10,8},{9,1... | collective-permute-start | bytes 147464 | tf_op jit(solution)/shard_map/ppermute | solution.py:446
  26.1 1.2 %collective-permute-start.6 = (bf16[1,4,32,128]{3,2,1,0:T(8,128)(2,1)S(1)}, bf16[1,4,32,128]{3,2,1,0:T(8,128)(2,1)S(1)}, u32[]{:S(2)}, u32[]{:S(2)}) collective-permute-start(bf16[1,4,32,128]{3,2,1,0:T(8,128)(2,1)S(1)} %get-tuple-element.59), channel_id=1, source_target_pairs={{0,4},{4,8},{8,12},{12,0},{1,5},{5,9},{9,13},{13,1},{2,6},{6,10},{... | collective-permute-start | bytes 98312 | tf_op jit(solution)/shard_map/ppermute | solution.py:444
  27.3 2.6 %collective-permute-start.7 = (bf16[1,4,32,128]{3,2,1,0:T(8,128)(2,1)S(1)}, bf16[1,4,32,128]{3,2,1,0:T(8,128)(2,1)S(1)}, u32[]{:S(2)}, u32[]{:S(2)}) collective-permute-start(bf16[1,4,32,128]{3,2,1,0:T(8,128)(2,1)S(1)} %get-tuple-element.60), channel_id=1, source_target_pairs={{0,12},{4,0},{8,4},{12,8},{1,13},{5,1},{9,5},{13,9},{2,14},{6,2},{... | collective-permute-start | bytes 98312 | tf_op jit(solution)/shard_map/ppermute | solution.py:443
  30.0 0.6 %collective-permute-done.10 = bf16[224,128]{1,0:T(8,128)(2,1)S(1)} collective-permute-done((bf16[224,128]{1,0:T(8,128)(2,1)S(1)}, bf16[224,128]{1,0:T(8,128)(2,1)S(1)}, u32[]{:S(2)}, u32[]{:S(2)}) %collective-permute-start.10) | collective-permute-done | bytes 57376 | tf_op jit(solution)/shard_map/ppermute | solution.py:455
  30.6 0.8 %collective-permute-start.11 = (bf16[224,128]{1,0:T(8,128)(2,1)S(1)}, bf16[224,128]{1,0:T(8,128)(2,1)S(1)}, u32[]{:S(2)}, u32[]{:S(2)}) collective-permute-start(bf16[224,128]{1,0:T(8,128)(2,1)S(1)} %add.11.mine), channel_id=1, source_target_pairs={{0,2},{2,0},{1,3},{3,1},{4,6},{6,4},{5,7},{7,5},{8,10},{10,8},{9,1... | collective-permute-start | bytes 172040 | tf_op jit(solution)/shard_map/ppermute | solution.py:457
  31.4 0.5 %collective-permute-done.6.from_lo = bf16[1,4,32,128]{3,2,1,0:T(8,128)(2,1)S(1)} collective-permute-done((bf16[1,4,32,128]{3,2,1,0:T(8,128)(2,1)S(1)}, bf16[1,4,32,128]{3,2,1,0:T(8,128)(2,1)S(1)}, u32[]{:S(2)}, u32[]{:S(2)}) %collective-permute-start.6) | collective-permute-done | bytes 32800 | tf_op jit(solution)/shard_map/ppermute | solution.py:444
  31.8 0.0 collective-permute-done.7.from_hi
  31.8 0.0 collective-permute-done.8.ig_from_lo.ig_from_hi
  31.9 0.8 %outputs.1 = (bf16[6,4,32,128]{3,2,1,0:T(8,128)(2,1)}, bf16[6,4,32,128]{3,2,1,0:T(8,128)(2,1)}) custom-call(f32[6,4,32,128]{3,2,1,0:T(8,128)S(1)} %get-tuple-element.53.own, bf16[1,4,32,128]{3,2,1,0:T(8,128)(2,1)S(1)} %collective-permute-done.6.from_lo, bf16[1,4,32,128]{3,2,1,0:T(8,128)(2,1)S(1)} %collective-permute-done.7.from_hi, ...), custom_call_target="tpu_custom_call" | custom-call | flops 536870912 | bytes 1048576 | tf_op jit(solution)/shard_map/outputs/pallas_call | solution.py:464
  32.7 2.2 %collective-permute-done.11.other = bf16[224,128]{1,0:T(8,128)(2,1)S(1)} collective-permute-done((bf16[224,128]{1,0:T(8,128)(2,1)S(1)}, bf16[224,128]{1,0:T(8,128)(2,1)S(1)}, u32[]{:S(2)}, u32[]{:S(2)}) %collective-permute-start.11) | collective-permute-done | bytes 57376 | tf_op jit(solution)/shard_map/ppermute | solution.py:457
  34.8 1.0 %unpack.1 = (f32[3,3,64,72]{3,2,1,0:T(8,128)}, f32[3,64,72]{2,1,0:T(8,128)}) custom-call(bf16[224,128]{1,0:T(8,128)(2,1)S(1)} %add.11.mine, bf16[224,128]{1,0:T(8,128)(2,1)S(1)} %collective-permute-done.11.other), custom_call_target="tpu_custom_call" | custom-call | tf_op jit(solution)/shard_map/unpack/pallas_call | solution.py:472
  (5 shorter events, 0.1 us)
Async XLA Ops:
  0.6 7.7 %copy-start = (bf16[6,4,64,128]{3,2,1,0:T(8,128)(2,1)S(1)}, bf16[6,4,64,128]{3,2,1,0:T(8,128)(2,1)}, u32[]{:S(2)}) copy-start(bf16[6,4,64,128]{3,2,1,0:T(8,128)(2,1)} %x.1) | copy-start | bytes 1179652
  0.6 7.7 %copy-start.1 = (bf16[6,4,64,128]{3,2,1,0:T(8,128)(2,1)S(1)}, bf16[6,4,64,128]{3,2,1,0:T(8,128)(2,1)}, u32[]{:S(2)}) copy-start(bf16[6,4,64,128]{3,2,1,0:T(8,128)(2,1)} %u.1) | copy-start | bytes 1179652
  2.2 9.0 %collective-permute-start.1 = (bf16[4,64,128]{2,1,0:T(8,128)(2,1)}, bf16[4,64,128]{2,1,0:T(8,128)(2,1)S(1)}, u32[]{:S(2)}, u32[]{:S(2)}) collective-permute-start(bf16[4,64,128]{2,1,0:T(8,128)(2,1)} %get-tuple-element.40), channel_id=1, source_target_pairs={{0,13},{1,4},{4,1},{5,8},{8,5},{9,12},{12,9},{13,0},{2,15},{3,6},{... | collective-permute-start | bytes 196616 | tf_op jit(solution)/shard_map/ppermute | solution.py:363
  6.8 4.5 %collective-permute-start = (bf16[3,64,128]{2,1,0:T(8,128)(2,1)}, bf16[3,64,128]{2,1,0:T(8,128)(2,1)S(1)}, u32[]{:S(2)}, u32[]{:S(2)}) collective-permute-start(bf16[3,64,128]{2,1,0:T(8,128)(2,1)} %get-tuple-element.39), channel_id=1, source_target_pairs={{0,2},{2,0},{1,3},{3,1},{4,6},{6,4},{5,7},{7,5},{8,10},{10,8},{9,1... | collective-permute-start | bytes 147464 | tf_op jit(solution)/shard_map/ppermute | solution.py:365
  8.3 0.9 %copy-start.2 = (bf16[3,3,64,72]{3,2,1,0:T(8,128)(2,1)S(1)}, bf16[3,3,64,72]{3,2,1,0:T(8,128)(2,1)}, u32[]{:S(2)}) copy-start(bf16[3,3,64,72]{3,2,1,0:T(8,128)(2,1)} %refs_4_.1) | copy-start | bytes 248836
  9.2 0.8 %copy-start.3 = (bf16[3,72,64]{1,2,0:T(8,128)(2,1)S(1)}, bf16[3,72,64]{1,2,0:T(8,128)(2,1)}, u32[]{:S(2)}) copy-start(bf16[3,72,64]{1,2,0:T(8,128)(2,1)} %param.6) | copy-start | bytes 82948
  11.3 1.4 %collective-permute-start.2 = (bf16[7,64,128]{2,1,0:T(8,128)(2,1)S(1)}, bf16[7,64,128]{2,1,0:T(8,128)(2,1)S(1)}, u32[]{:S(2)}, u32[]{:S(2)}) collective-permute-start(bf16[7,64,128]{2,1,0:T(8,128)(2,1)S(1)} %pad_maximum_fusion), channel_id=1, source_target_pairs={{0,1},{1,0},{2,3},{3,2},{4,5},{5,4},{6,7},{7,6},{8,9},{9,8},{10,11... | collective-permute-start | bytes 344072 | tf_op jit(solution)/shard_map/ppermute | solution.py:395
  11.4 4.0 %collective-permute-start.3 = (bf16[3,3,64,72]{3,2,1,0:T(8,128)(2,1)S(1)}, bf16[3,3,64,72]{3,2,1,0:T(8,128)(2,1)S(1)}, u32[]{:S(2)}, u32[]{:S(2)}) collective-permute-start(bf16[3,3,64,72]{3,2,1,0:T(8,128)(2,1)S(1)} %copy-done.2), channel_id=1, source_target_pairs={{0,1},{1,0},{2,3},{3,2},{4,5},{5,4},{6,7},{7,6},{8,9},{9,8},{10,11... | collective-permute-start | bytes 248840 | tf_op jit(solution)/shard_map/ppermute | solution.py:368
  11.9 3.5 %collective-permute-start.4 = (bf16[3,64,72]{2,1,0:T(8,128)(2,1)S(1)}, bf16[3,64,72]{2,1,0:T(8,128)(2,1)S(1)}, u32[]{:S(2)}, u32[]{:S(2)}) collective-permute-start(bf16[3,64,72]{2,1,0:T(8,128)(2,1)S(1)} %bitcast.3), channel_id=1, source_target_pairs={{0,1},{1,0},{2,3},{3,2},{4,5},{5,4},{6,7},{7,6},{8,9},{9,8},{10,11... | collective-permute-start | bytes 82952 | tf_op jit(solution)/shard_map/ppermute | solution.py:369
  14.0 6.3 %collective-permute-start.5 = (bf16[224,128]{1,0:T(8,128)(2,1)S(1)}, bf16[224,128]{1,0:T(8,128)(2,1)S(1)}, u32[]{:S(2)}, u32[]{:S(2)}) collective-permute-start(bf16[224,128]{1,0:T(8,128)(2,1)S(1)} %get-tuple-element.54), channel_id=1, source_target_pairs={{0,2},{2,0},{1,3},{3,1},{4,6},{6,4},{5,7},{7,5},{8,10},{10,8},{9,1... | collective-permute-start | bytes 172040 | tf_op jit(solution)/shard_map/ppermute | solution.py:416
  20.4 4.2 %collective-permute-start.9 = (bf16[224,128]{1,0:T(8,128)(2,1)S(1)}, bf16[224,128]{1,0:T(8,128)(2,1)S(1)}, u32[]{:S(2)}, u32[]{:S(2)}) collective-permute-start(bf16[224,128]{1,0:T(8,128)(2,1)S(1)} %add_convert_fusion), channel_id=1, source_target_pairs={{0,4},{4,0},{8,12},{12,8},{1,5},{5,1},{9,13},{13,9},{2,6},{6,2},{1... | collective-permute-start | bytes 172040 | tf_op jit(solution)/shard_map/ppermute | solution.py:455
  24.7 5.9 %collective-permute-start.10 = (bf16[224,128]{1,0:T(8,128)(2,1)S(1)}, bf16[224,128]{1,0:T(8,128)(2,1)S(1)}, u32[]{:S(2)}, u32[]{:S(2)}) collective-permute-start(bf16[224,128]{1,0:T(8,128)(2,1)S(1)} %add.10), channel_id=1, source_target_pairs={{0,8},{4,12},{8,0},{12,4},{1,9},{5,13},{9,1},{13,5},{2,10},{6,14},... | collective-permute-start | bytes 172040 | tf_op jit(solution)/shard_map/ppermute | solution.py:455
  24.8 7.1 %collective-permute-start.8 = (bf16[6,32,128]{2,1,0:T(8,128)(2,1)S(1)}, bf16[6,32,128]{2,1,0:T(8,128)(2,1)S(1)}, u32[]{:S(2)}, u32[]{:S(2)}) collective-permute-start(bf16[6,32,128]{2,1,0:T(8,128)(2,1)S(1)} %broadcast_select_fusion), channel_id=1, source_target_pairs={{0,2},{2,0},{1,3},{3,1},{4,6},{6,4},{5,7},{7,5},{8,10},{10,8},{9,1... | collective-permute-start | bytes 147464 | tf_op jit(solution)/shard_map/ppermute | solution.py:446
  26.1 5.7 %collective-permute-start.6 = (bf16[1,4,32,128]{3,2,1,0:T(8,128)(2,1)S(1)}, bf16[1,4,32,128]{3,2,1,0:T(8,128)(2,1)S(1)}, u32[]{:S(2)}, u32[]{:S(2)}) collective-permute-start(bf16[1,4,32,128]{3,2,1,0:T(8,128)(2,1)S(1)} %get-tuple-element.59), channel_id=1, source_target_pairs={{0,4},{4,8},{8,12},{12,0},{1,5},{5,9},{9,13},{13,1},{2,6},{6,10},{... | collective-permute-start | bytes 98312 | tf_op jit(solution)/shard_map/ppermute | solution.py:444
  27.3 4.5 %collective-permute-start.7 = (bf16[1,4,32,128]{3,2,1,0:T(8,128)(2,1)S(1)}, bf16[1,4,32,128]{3,2,1,0:T(8,128)(2,1)S(1)}, u32[]{:S(2)}, u32[]{:S(2)}) collective-permute-start(bf16[1,4,32,128]{3,2,1,0:T(8,128)(2,1)S(1)} %get-tuple-element.60), channel_id=1, source_target_pairs={{0,12},{4,0},{8,4},{12,8},{1,13},{5,1},{9,5},{13,9},{2,14},{6,2},{... | collective-permute-start | bytes 98312 | tf_op jit(solution)/shard_map/ppermute | solution.py:443
  30.6 4.2 %collective-permute-start.11 = (bf16[224,128]{1,0:T(8,128)(2,1)S(1)}, bf16[224,128]{1,0:T(8,128)(2,1)S(1)}, u32[]{:S(2)}, u32[]{:S(2)}) collective-permute-start(bf16[224,128]{1,0:T(8,128)(2,1)S(1)} %add.11.mine), channel_id=1, source_target_pairs={{0,2},{2,0},{1,3},{3,1},{4,6},{6,4},{5,7},{7,5},{8,10},{10,8},{9,1... | collective-permute-start | bytes 172040 | tf_op jit(solution)/shard_map/ppermute | solution.py:457
where the time goes:
time: 36 us; the launch traced here: 35.8 us
  starting transfers between devices  14.2 us (39%)
  Pallas kernels  10.9 us (30%)
  waiting for transfers between devices  8.18 us (23%)
  local copies, waits for them, and re-layouts  1.72 us (5%)
  between operations  0.76 us (2%)
    pallas_call x1, Pallas kernels, shards(): call(functools.partial(fields_kernel, dims), 'field_products', [sds(own_s...  4.95 us
    ppermute x2, waiting for transfers between devices, shards(): lax.ppermute(mine, 'tm', pairs(tm_count, stride))  4.77 us
    ppermute x1, starting transfers between devices, shards(): frame = lax.ppermute(frame, ('tm', 'chan'), facing(tm_count))  4.55 us
    ppermute x1, starting transfers between devices, shards(): from_hi = lax.ppermute(out_lo, 'tm', ring(tm_count, -1))  2.61 us
    ppermute x1, waiting for transfers between devices, shards(): other = lax.ppermute(mine, 'axial', ring(2, 1))  2.18 us
    unnamed x8, local copies, waits for them, and re-layouts  1.72 us
    pallas_call x1, Pallas kernels, shards(): call(functools.partial(stage_kernel, split), 'stage', [sds((edge_count, c...  1.58 us
    ppermute x1, starting transfers between devices, shards(): edge = lax.ppermute(edge, 'axial', ring(2, 1))  1.49 us
  transfers between devices with their start and end apart: 12, of which 5 were waited for; matrix products, arithmetic and copies ran while one was open for 0% of the time, Pallas kernels for 23%

commit v1 on v0

--- a/solution.py
+++ b/solution.py
@@ -60,6 +60,16 @@
             blocks.append((row, g * rest, g * part, total - rest, part, rest))
         row += part
     return blocks, row
+
+
+def padded(count):
+    return -(-count // 16) * 16
+
+
+def with_rows(value, count):
+    if value.shape[0] == count:
+        return value
+    return jnp.concatenate([value, jnp.zeros((count - value.shape[0], value.shape[1]), value.dtype)], 0)
 
 
 def half_rows(depth, total):
@@ -138,15 +148,15 @@
                 0,
             ).astype(BF16)
         )
-        hids = [v.astype(BF16) for v in hids]
+        hids = [with_rows(v, padded(v.shape[0])).astype(BF16) for v in hids]
         owns.append(jnp.concatenate(hids, 1))
         for f, hid, grad in zip(picked, hids, grads):
-            store(h, f, hid, grad.astype(BF16))
+            store(h, f, hid, with_rows(grad, padded(grad.shape[0])).astype(BF16))
         fields.append(field)
         cots.append(cot)
     return (
         dot_nt(jnp.concatenate(fields, 1), jnp.concatenate(shifts, 1)),
-        dot_nt(jnp.concatenate(cots, 1), jnp.concatenate(owns, 1)),
+        dot_nt(jnp.concatenate(cots, 1), jnp.concatenate(owns, 1))[:, : w_act.shape[0]],
     )
 
 
@@ -181,7 +191,7 @@
 def grads_kernel(dims, *refs):
     frames, rows, channels, width, mid, own_c, rank_count, axial_count, group = dims
     hid_in, grad_in, acc_in, x, u, edge, frame, swapped, taps_in, act_in = refs[:10]
-    hid_out, grad_out, xp, up, keep, send, edges, acc, packed = refs[10:]
+    hid_out, grad_out, xp, up, half_0, half_1, edges, acc, packed = refs[10:]
     axial = lax.axis_index("axial")
     core = lax.axis_index("chan")
     w_taps, w_act = taps_in[...], act_in[...]
@@ -222,70 +232,96 @@
     packed[used:] = jnp.zeros((2 * size - used, LANES), F32)
     for at, lane, source, column, depth, total in blocks:
         packed[at : at + depth, lane : lane + total] = acc[source : source + depth, column : column + total]
-    mine = lax.rem(axial, 2)
-    keep[...] = packed[pl.ds(pl.multiple_of(mine * size, 16), size)]
-    send[...] = packed[pl.ds(pl.multiple_of((1 - mine) * size, 16), size)].astype(send.dtype)
-
-
-def fields_kernel(dims, *refs):
+    half_0[...] = packed[:size].astype(half_0.dtype)
+    half_1[...] = packed[size:].astype(half_1.dtype)
+
+
+def others_kernel(dims, *refs):
     frames, rows, channels, width, mid, own_c, rank_count, axial_count, group = dims
-    hid_in, grad_in, xp, up, sw, tw, sw_other, tw_other = refs[:8]
-    out, out_lo, out_hi, ig, ig_lo, ig_hi, wf, twf, twt, wg, ig_acc = refs[8:]
-    core = lax.axis_index("chan")
-    first_c = pl.multiple_of(core * own_c, own_c)
-    own = pl.ds(first_c, own_c)
-    w_taps, w_act = prepare(sw_other, tw_other, wf, twf)
+    xp, up, sw, tw, hid_out, grad_out, wf, twf = refs
+    w_taps, w_act = prepare(sw, tw, wf, twf)
+    for h in range(rows):
+        for first in range(0, frames, group):
+            picked = range(first, first + group)
+            field, cot = gathered(xp, up, h, picked)
+            for f, hid, grad in zip(picked, *activations(w_taps, w_act, field, cot, width)):
+                hid_out[h, f] = with_rows(hid, padded(mid)).astype(BF16)
+                grad_out[h, f] = with_rows(grad, padded(mid)).astype(BF16)
+
+
+def fields_kernel(dims, fast, *refs):
+    frames, rows, channels, width, mid, own_c, rank_count, axial_count, group = dims
+    hid_in, grad_in, hid_other, grad_other, sw, tw, sw_other, tw_other = refs[:8]
+    out, out_a, out_b, ig, ig_a, ig_b, twt, wg, ig_acc, out_edges = refs[8:]
+    own = pl.ds(pl.multiple_of(lax.axis_index("chan") * own_c, own_c), own_c)
+    blank = jnp.zeros((own_c, padded(mid) - mid), F32)
+
+    def both(a, b):
+        return jnp.concatenate([a.astype(F32), blank, b.astype(F32), blank], 1).astype(BF16)
+
     for k in range(3):
-        twt[k * own_c : (k + 1) * own_c] = jnp.concatenate(
-            [w[k, own].astype(F32) for w in (tw, tw_other)], 1
-        ).astype(BF16)
+        twt[k * own_c : (k + 1) * own_c] = both(tw[k, own], tw_other[k, own])
     for i in range(3):
         for j in range(3):
             at = (i * 3 + j) * own_c
-            wg[at : at + own_c] = jnp.concatenate([w[i, j, own].astype(F32) for w in (sw, sw_other)], 1).astype(BF16)
-    ig_acc[...] = jnp.zeros_like(ig_acc)
-
-    def row(h, carry):
+            wg[at : at + own_c] = both(sw[i, j, own], sw_other[i, j, own])
+    w_out, w_in = twt[...], wg[...]
+
+    for h in range(rows):
         out_terms = {}
         for first in range(0, frames, group):
-            field, cot = gathered(xp, up, h, range(first, first + group))
-            hids, grads = activations(w_taps, w_act, field, cot, width)
             picked = range(first, first + group)
-            hid = [jnp.concatenate([hid_in[h, f].astype(F32), v], 0) for f, v in zip(picked, hids)]
-            grad = [jnp.concatenate([grad_in[h, f].astype(F32), v], 0) for f, v in zip(picked, grads)]
-            y_out = dot(twt[...], jnp.concatenate(hid, 1).astype(BF16))
-            y_in = dot(wg[...], jnp.concatenate(grad, 1).astype(BF16))
-            for g in range(group):
-                f = first + g
+            hid = jnp.concatenate([jnp.concatenate([hid_in[h, f], hid_other[h, f]], 0) for f in picked], 1)
+            grad = jnp.concatenate([jnp.concatenate([grad_in[h, f], grad_other[h, f]], 0) for f in picked], 1)
+            y_out = dot(w_out, hid)
+            y_in = dot(w_in, grad)
+            for g, f in enumerate(picked):
                 cols = slice(g * width, (g + 1) * width)
                 for k in range(3):
                     out_terms.setdefault(f - k + 1, []).append(y_out[k * own_c : (k + 1) * own_c, cols])
                 for i in range(3):
                     at = i * 3 * own_c
-                    ig_acc[f, h + i] += (
+                    total = (
                         y_in[at + own_c : at + 2 * own_c, cols]
                         + moved(y_in[at : at + own_c, cols], -1)
                         + moved(y_in[at + 2 * own_c : at + 3 * own_c, cols], 1)
                     )
+                    if h == 0 or i == 2:
+                        ig_acc[f, h + i] = total
+                    else:
+                        ig_acc[f, h + i] += total
         for f, terms in out_terms.items():
             total = functools.reduce(lambda a, b: a + b, terms)
             if f < 0:
-                out_lo[0, h] = total.astype(BF16)
+                out_edges[0, h] = total.astype(BF16)
             elif f >= frames:
-                out_hi[0, h] = total.astype(BF16)
+                out_edges[1, h] = total.astype(BF16)
             else:
                 out[f, h] = total
-        return carry
-
-    lax.fori_loop(0, rows, row, 0)
+
+    odd = lax.rem(lax.axis_index("tm"), 2) if fast else 1
+    high = jnp.where(lax.axis_index("axial") == 0, rows + 1, 0) if fast else 0
+    out_a[...] = out_edges[1 - odd]
+    out_b[...] = out_edges[odd]
     for f in range(frames):
-        ig_lo[f] = ig_acc[f, 0].astype(BF16)
-        ig_hi[f] = ig_acc[f, rows + 1].astype(BF16)
+        ig_a[f] = ig_acc[f, high].astype(BF16)
+        ig_b[f] = ig_acc[f, rows + 1].astype(BF16)
         for h in range(rows):
             ig[f, h] = ig_acc[f, h + 1]
 
 
-def outputs_kernel(axial_count, own, from_lo, from_hi, ig_own, ig_from_lo, ig_from_hi, out, ig):
+def unpack(packed, acc, sg, tg):
+    channels, mid = tg.shape[1:]
+    for at, lane, source, column, depth, total in pieces(*acc.shape)[0]:
+        acc[source : source + depth, column : column + total] = packed[at : at + depth, lane : lane + total]
+    for i in range(3):
+        rows = slice(i * channels, (i + 1) * channels)
+        for j in range(3):
+            sg[i, j] = acc[rows, j * mid : (j + 1) * mid]
+        tg[2 - i] = acc[rows, 3 * mid :]
+
+
+def add_edges(axial_count, own, from_lo, from_hi, ig_own, ig_from_lo, ig_from_hi, out, ig):
     frames, rows = own.shape[:2]
     axial = lax.axis_index("axial")
     has_lo = (axial > 0).astype(F32)
@@ -294,31 +330,57 @@
         for h in range(rows):
             total = own[f, h]
             if f == 0:
-                total = total + from_lo[0, h].astype(F32)
+                total = total + from_lo(h).astype(F32)
             if f == frames - 1:
-                total = total + from_hi[0, h].astype(F32)
+                total = total + from_hi(h).astype(F32)
             out[f, h] = total.astype(BF16)
             total = ig_own[f, h]
             if h == 0:
-                total = total + ig_from_lo[f].astype(F32) * has_lo
+                total = total + ig_from_lo(f).astype(F32) * has_lo
             if h == rows - 1:
-                total = total + ig_from_hi[f].astype(F32) * has_hi
+                total = total + ig_from_hi(f).astype(F32) * has_hi
             ig[f, h] = total.astype(BF16)
 
 
-def unpack_kernel(mine, other, sg, tg, packed, acc):
-    channels, mid = tg.shape[1:]
-    size = mine.shape[0]
-    half = lax.rem(lax.axis_index("axial"), 2)
-    packed[pl.ds(pl.multiple_of(half * size, 16), size)] = mine[...].astype(F32)
-    packed[pl.ds(pl.multiple_of((1 - half) * size, 16), size)] = other[...].astype(F32)
-    for at, lane, source, column, depth, total in pieces(*acc.shape)[0]:
-        acc[source : source + depth, column : column + total] = packed[at : at + depth, lane : lane + total]
-    for i in range(3):
-        rows = slice(i * channels, (i + 1) * channels)
-        for j in range(3):
-            sg[i, j] = acc[rows, j * mid : (j + 1) * mid]
-        tg[2 - i] = acc[rows, 3 * mid :]
+def last_kernel(own, ig_own, half_0, got_0, half_1, got_1, got_a, out, ig, sg, tg, packed, acc, edges):
+    frames, rows, own_c, width = own.shape
+    size = half_0.shape[0]
+    odd = lax.rem(lax.axis_index("tm"), 2)
+    edges[1 - odd] = got_a[...]
+    edges[odd] = got_1[size:].reshape(rows, own_c, width)
+    add_edges(
+        2,
+        own,
+        lambda h: edges[0, h],
+        lambda h: edges[1, h],
+        ig_own,
+        lambda f: got_0[size + f * own_c : size + (f + 1) * own_c],
+        lambda f: got_0[size + f * own_c : size + (f + 1) * own_c],
+        out,
+        ig,
+    )
+    packed[:size] = half_0[...].astype(F32) + got_0[:size].astype(F32)
+    packed[size:] = half_1[...].astype(F32) + got_1[:size].astype(F32)
+    unpack(packed, acc, sg, tg)
+
+
+def last_kernel_general(axial_count, *refs):
+    own, ig_own, half_0, half_1, from_lo, from_hi, ig_from_lo, ig_from_hi, out, ig, sg, tg, packed, acc, edges = refs
+    add_edges(
+        axial_count,
+        own,
+        lambda h: from_lo[h],
+        lambda h: from_hi[h],
+        ig_own,
+        lambda f: ig_from_lo[f],
+        lambda f: ig_from_hi[f],
+        out,
+        ig,
+    )
+    size = half_0.shape[0]
+    packed[:size] = half_0[...]
+    packed[size:] = half_1[...]
+    unpack(packed, acc, sg, tg)
 
 
 def call(kernel, name, out_shape, count, limit, scratch=(), in_specs=None, flops=0):
@@ -369,11 +431,13 @@
     tw_other = lax.ppermute(turned, "chan", ring(2, 1))
 
     own_shape = (frames, rows, own_c, width)
-    inner = (inner_rows(axial_count, rows)[1], frames - 2, mid, width)
-    cells = (rows, frames, mid, width)
+    inner = (inner_rows(axial_count, rows)[1], frames - 2, padded(mid), width)
+    cells = (rows, frames, padded(mid), width)
     xp_shape = (frames, rows + 2, channels, width)
     up_shape = (frames + 2, rows, channels, width)
     total = (3 * channels, 4 * mid)
+    forms = [pltpu.VMEM((3 * mid, 3 * channels), F32), pltpu.VMEM((mid, 3 * channels), F32)]
+    fast = axial_count == 2 and tm_count == 4
     hid, grad, acc, xp, up, w_taps, w_act = call(
         functools.partial(inner_kernel, dims),
         "inner_cells",
@@ -388,12 +452,13 @@
         ],
         4,
         16,
-        [pltpu.VMEM((3 * mid, 3 * channels), F32), pltpu.VMEM((mid, 3 * channels), F32)],
+        forms,
         flops=1 << 31,
     )(frames_in, upstream, spatial_weight, turned)
     edge, frame, acc = lax.optimization_barrier((edge, frame, acc))
     swapped = lax.ppermute(jnp.concatenate([edge, frame], 0), "chan", ring(2, 1))
-    hid, grad, xp, up, keep, send = call(
+    half_type = BF16 if fast else F32
+    hid, grad, xp, up, half_0, half_1 = call(
         functools.partial(grads_kernel, dims),
         "weight_grads",
         [
@@ -401,8 +466,8 @@
             sds(cells, BF16),
             sds(xp_shape, BF16),
             sds(up_shape, BF16),
-            sds((size, LANES), F32),
-            sds((size, LANES), BF16 if axial_count == 2 else F32),
+            sds((size, LANES), half_type),
+            sds((size, LANES), half_type),
         ],
         10,
         16,
@@ -413,70 +478,74 @@
         ],
     )(hid, grad, acc, xp, up, edge, frame, swapped, w_taps, w_act)
 
-    got = lax.ppermute(send, "axial", ring(2, 1)) if axial_count == 2 else None
-
-    out_own, out_lo, out_hi, ig_own, ig_lo, ig_hi = call(
-        functools.partial(fields_kernel, dims),
+    if fast:
+        near, far = pairs(4, 1), [(0, 3), (1, 2), (2, 1), (3, 0)]
+        got_0 = lax.ppermute(half_0, "tm", near)
+        got_1 = lax.ppermute(half_1, "axial", ring(2, 1))
+
+    hid_other, grad_other = call(
+        functools.partial(others_kernel, dims),
+        "other_cells",
+        [sds(cells, BF16), sds(cells, BF16)],
+        4,
+        16,
+        forms,
+        flops=1 << 31,
+    )(xp, up, sw_other, tw_other)
+
+    if fast:
+        got_0, got_1, hid_other = lax.optimization_barrier((got_0, got_1, hid_other))
+        half_0, half_1 = lax.optimization_barrier((half_0 + got_0, half_1 + got_1))
+        got_0 = lax.ppermute(half_0, "tm", pairs(4, 2))
+        got_1 = lax.ppermute(half_1, "tm", near)
+
+    own_shape = (frames, rows, own_c, width)
+    out_edge, ig_edge = sds((rows, own_c, width), BF16), sds((frames, own_c, width), BF16)
+    out_own, out_a, out_b, ig_own, ig_a, ig_b = call(
+        functools.partial(fields_kernel, dims, fast),
         "field_products",
-        [
-            sds(own_shape, F32),
-            sds((1, rows, own_c, width), BF16),
-            sds((1, rows, own_c, width), BF16),
-            sds(own_shape, F32),
-            sds((frames, own_c, width), BF16),
-            sds((frames, own_c, width), BF16),
-        ],
+        [sds(own_shape, F32), out_edge, out_edge, sds(own_shape, F32), ig_edge, ig_edge],
         8,
         16,
         [
-            pltpu.VMEM((3 * mid, 3 * channels), F32),
-            pltpu.VMEM((mid, 3 * channels), F32),
-            pltpu.VMEM((3 * own_c, 2 * mid), BF16),
-            pltpu.VMEM((9 * own_c, 2 * mid), BF16),
+            pltpu.VMEM((3 * own_c, 2 * padded(mid)), BF16),
+            pltpu.VMEM((9 * own_c, 2 * padded(mid)), BF16),
             pltpu.VMEM((frames, rows + 2, own_c, width), F32),
+            pltpu.VMEM((2, rows, own_c, width), BF16),
         ],
         flops=1 << 31,
-    )(hid, grad, xp, up, spatial_weight, turned, sw_other, tw_other)
-    if got is not None:
-        got, out_lo, out_hi, ig_lo, ig_hi = lax.optimization_barrier((got, out_lo, out_hi, ig_lo, ig_hi))
-
-    from_hi = lax.ppermute(out_lo, "tm", ring(tm_count, -1))
-    from_lo = lax.ppermute(out_hi, "tm", ring(tm_count, 1))
-    if axial_count == 2:
-        ig_from_lo = ig_from_hi = lax.ppermute(jnp.where(axial == 0, ig_hi, ig_lo), "axial", ring(2, 1))
+    )(hid, grad, hid_other, grad_other, spatial_weight, turned, sw_other, tw_other)
+
+    outs = [
+        sds(own_shape, BF16),
+        sds(own_shape, BF16),
+        sds((3, 3, channels, mid), F32),
+        sds((3, channels, mid), F32),
+    ]
+    scratch = [
+        pltpu.VMEM((2 * size, LANES), F32),
+        pltpu.VMEM(total, F32),
+        pltpu.VMEM((2, rows, own_c, width), BF16),
+    ]
+    if fast:
+        got_0, got_1, out_a, out_b, ig_a = lax.optimization_barrier((got_0, got_1, out_a, out_b, ig_a))
+        half_0, half_1 = lax.optimization_barrier((half_0 + got_0, half_1 + got_1))
+        got_1 = lax.ppermute(jnp.concatenate([half_1, out_b.reshape(-1, width)], 0), "tm", far)
+        got_0 = lax.ppermute(jnp.concatenate([half_0, ig_a.reshape(-1, width)], 0), "axial", ring(2, 1))
+        got_a = lax.ppermute(out_a, "tm", near)
+        results = call(last_kernel, "last", outs, 7, 8, scratch)(
+            out_own, ig_own, half_0, got_0, half_1, got_1, got_a
+        )
     else:
-        ig_from_hi = lax.ppermute(ig_lo, "axial", ring(axial_count, -1))
-        ig_from_lo = lax.ppermute(ig_hi, "axial", ring(axial_count, 1))
-
-    if axial_count == 2 and tm_count & (tm_count - 1) == 0:
-        mine = lax.optimization_barrier((keep + got.astype(F32)).astype(BF16))
-        stride = 1
-        while stride < tm_count:
-            mine = lax.optimization_barrier(mine + lax.ppermute(mine, "tm", pairs(tm_count, stride)))
-            stride *= 2
-        other = lax.ppermute(mine, "axial", ring(2, 1))
-    else:
-        odd = lax.rem(axial, 2) == 1
-        low, high = jnp.where(odd, send, keep), jnp.where(odd, keep, send)
-        low, high = lax.psum((low, high), ("tm", "axial"))
-        mine, other = jnp.where(odd, high, low), jnp.where(odd, low, high)
-
-    output, input_grad = call(
-        functools.partial(outputs_kernel, axial_count),
-        "outputs",
-        [sds(own_shape, BF16), sds(own_shape, BF16)],
-        6,
-        4,
-        flops=1 << 29,
-    )(out_own, from_lo, from_hi, ig_own, ig_from_lo, ig_from_hi)
-    spatial_grad, temporal_grad = call(
-        unpack_kernel,
-        "unpack",
-        [sds((3, 3, channels, mid), F32), sds((3, channels, mid), F32)],
-        2,
-        4,
-        [pltpu.VMEM((2 * size, LANES), F32), pltpu.VMEM((3 * channels, 4 * mid), F32)],
-    )(mine, other)
+        half_0, half_1 = lax.psum((half_0, half_1), ("tm", "axial"))
+        from_hi = lax.ppermute(out_a, "tm", ring(tm_count, -1))
+        from_lo = lax.ppermute(out_b, "tm", ring(tm_count, 1))
+        ig_from_hi = lax.ppermute(ig_a, "axial", ring(axial_count, -1))
+        ig_from_lo = lax.ppermute(ig_b, "axial", ring(axial_count, 1))
+        results = call(functools.partial(last_kernel_general, axial_count), "last", outs, 8, 8, scratch)(
+            out_own, ig_own, half_0, half_1, from_lo, from_hi, ig_from_lo, ig_from_hi
+        )
+    output, input_grad, spatial_grad, temporal_grad = results
     return output, input_grad, spatial_grad, jnp.swapaxes(temporal_grad, 1, 2)
 
 

time: 36 us -> 34 us (0.944)
  Pallas kernels: 10.9 us -> 7.6 us
  waiting for transfers between devices: 8.18 us -> 8.7 us
  starting transfers between devices: 14.2 us -> 14.6 us
    pallas_call x3, Pallas kernels: 6.73 us -> 3.48 us  [the longest x1 1.57 us: shards(): call(functools.partial(fields_kernel, dims, fast), 'field_products', [sds...]
    ppermute x7, waiting for transfers between devices: 7.43 us -> 8.07 us  [the longest x1 4.29 us: shards(): got_a = lax.ppermute(out_a, 'tm', near)]
    ppermute x7, starting transfers between devices: 7.49 us -> 8.03 us  [the longest x1 2.38 us: shards(): lax.ppermute(jnp.concatenate([half_1, out_b.reshape(-1, width)], 0), 'tm'...]
    unnamed x8 -> x10, local copies, waits for them, and re-layouts: 1.72 us -> 1.91 us
  transfers between devices with their start and end apart: 12 -> 12, of which waited for: 5 -> 6; matrix products, arithmetic and copies ran while one was open for 0% -> 0% of each run, Pallas kernels for 23% -> 15%
where the time goes in v1:
time: 34 us; the launch traced here: 33.7 us
  starting transfers between devices  14.6 us (43%)
  waiting for transfers between devices  8.7 us (26%)
  Pallas kernels  7.6 us (22%)
  local copies, waits for them, and re-layouts  1.91 us (6%)
  between operations  0.76 us (2%)
    ppermute x1, starting transfers between devices, shards(): frame = lax.ppermute(frame, ('tm', 'chan'), facing(tm_count))  4.55 us
    ppermute x1, waiting for transfers between devices, shards(): got_a = lax.ppermute(out_a, 'tm', near)  4.29 us
    ppermute x1, starting transfers between devices, shards(): lax.ppermute(jnp.concatenate([half_1, out_b.reshape(-1, width)], 0), 'tm'...  2.38 us
    ppermute x1, waiting for transfers between devices, shards(): got_0 = lax.ppermute(half_0, 'tm', near)  1.92 us
    unnamed x10, local copies, waits for them, and re-layouts  1.91 us
    ppermute x1, starting transfers between devices, shards(): got_0 = lax.ppermute(half_0, 'tm', pairs(4, 2))  1.8 us
    pallas_call x1, Pallas kernels, shards(): call(functools.partial(stage_kernel, split), 'stage', [sds((edge_count, c...  1.58 us
    pallas_call x1, Pallas kernels, shards(): call(functools.partial(fields_kernel, dims, fast), 'field_products', [sds...  1.57 us
  transfers between devices with their start and end apart: 12, of which 6 were waited for; matrix products, arithmetic and copies ran while one was open for 0% of the time, Pallas kernels for 15%

profile of v1, /device:TPU:0, one launch (start us, length us, event | category | flops | bytes accessed | tf_op | source)
XLA Modules:
  0.0 33.7 jit_solution(18223035525552491237)
XLA Ops:
  0.6 0.0 copy-start
  0.6 0.0 copy-start.1
  0.7 1.6 %stage.1 = (bf16[3,64,128]{2,1,0:T(8,128)(2,1)}, bf16[4,64,128]{2,1,0:T(8,128)(2,1)}) custom-call(bf16[6,4,64,128]{3,2,1,0:T(8,128)(2,1)} %x.1, bf16[6,4,64,128]{3,2,1,0:T(8,128)(2,1)} %u.1), custom_call_target="tpu_custom_call" | custom-call | tf_op jit(solution)/shard_map/stage/pallas_call | solution.py:416
  2.2 4.6 %collective-permute-start.1 = (bf16[4,64,128]{2,1,0:T(8,128)(2,1)}, bf16[4,64,128]{2,1,0:T(8,128)(2,1)S(1)}, u32[]{:S(2)}, u32[]{:S(2)}) collective-permute-start(bf16[4,64,128]{2,1,0:T(8,128)(2,1)} %get-tuple-element.48), channel_id=1, source_target_pairs={{0,13},{1,4},{4,1},{5,8},{8,5},{9,12},{12,9},{13,0},{2,15},{3,6},{... | collective-permute-start | bytes 196616 | tf_op jit(solution)/shard_map/ppermute | solution.py:425
  6.8 1.5 %collective-permute-start = (bf16[3,64,128]{2,1,0:T(8,128)(2,1)}, bf16[3,64,128]{2,1,0:T(8,128)(2,1)S(1)}, u32[]{:S(2)}, u32[]{:S(2)}) collective-permute-start(bf16[3,64,128]{2,1,0:T(8,128)(2,1)} %get-tuple-element.47), channel_id=1, source_target_pairs={{0,2},{2,0},{1,3},{3,1},{4,6},{6,4},{5,7},{7,5},{8,10},{10,8},{9,1... | collective-permute-start | bytes 147464 | tf_op jit(solution)/shard_map/ppermute | solution.py:427
  8.3 0.0 copy-done
  8.3 0.0 copy-done.1
  8.3 0.0 copy-start.2
  8.3 0.9 %copy-done.2 = bf16[3,3,64,72]{3,2,1,0:T(8,128)(2,1)S(1)} copy-done((bf16[3,3,64,72]{3,2,1,0:T(8,128)(2,1)S(1)}, bf16[3,3,64,72]{3,2,1,0:T(8,128)(2,1)}, u32[]{:S(2)}) %copy-start.2) | copy-done | bytes 82968
  9.2 0.0 copy-start.3
  9.2 0.8 %copy-done.3 = bf16[3,72,64]{1,2,0:T(8,128)(2,1)S(1)} copy-done((bf16[3,72,64]{1,2,0:T(8,128)(2,1)S(1)}, bf16[3,72,64]{1,2,0:T(8,128)(2,1)}, u32[]{:S(2)}) %copy-start.3) | copy-done | bytes 27672
  10.0 1.2 %inner_cells.1 = (bf16[3,4,80,128]{3,2,1,0:T(8,128)(2,1)S(1)}, bf16[3,4,80,128]{3,2,1,0:T(8,128)(2,1)S(1)}, f32[192,288]{1,0:T(8,128)S(1)}, bf16[6,6,64,128]{3,2...) custom-call(bf16[6,4,64,128]{3,2,1,0:T(8,128)(2,1)S(1)} %copy-done, ...), custom_call_target="tpu_custom_call" | custom-call | flops 2147483648 | bytes 1048576 | tf_op jit(solution)/shard_map/inner_cells/pallas_call | solution.py:441
  11.3 0.0 collective-permute-done.refs_5_
  11.3 0.0 collective-permute-done.1.refs_6_
  11.3 0.0 copy-start.4
  11.3 0.1 collective-permute-start.2
  11.4 0.5 %collective-permute-start.5 = (bf16[3,3,64,72]{3,2,1,0:T(8,128)(2,1)S(1)}, bf16[3,3,64,72]{3,2,1,0:T(8,128)(2,1)S(1)}, u32[]{:S(2)}, u32[]{:S(2)}) collective-permute-start(bf16[3,3,64,72]{3,2,1,0:T(8,128)(2,1)S(1)} %copy-done.2), channel_id=1, source_target_pairs={{0,1},{1,0},{2,3},{3,2},{4,5},{5,4},{6,7},{7,6},{8,9},{9,8},{10,11... | collective-permute-start | bytes 248840 | tf_op jit(solution)/shard_map/ppermute | solution.py:430
  11.9 0.2 copy-done.4
  12.1 0.0 collective-permute-start.6
  12.1 0.6 %collective-permute-done.2.refs_7_ = bf16[7,64,128]{2,1,0:T(8,128)(2,1)S(1)} collective-permute-done((bf16[7,64,128]{2,1,0:T(8,128)(2,1)S(1)}, bf16[7,64,128]{2,1,0:T(8,128)(2,1)S(1)}, u32[]{:S(2)}, u32[]{:S(2)}) %collective-permute-start.2) | collective-permute-done | bytes 114720 | tf_op jit(solution)/shard_map/ppermute | solution.py:459
  12.7 1.3 %weight_grads.1 = (bf16[4,6,80,128]{3,2,1,0:T(8,128)(2,1)S(1)}, bf16[4,6,80,128]{3,2,1,0:T(8,128)(2,1)S(1)}, bf16[6,6,64,128]{3,2,1,0:T(8,128)(2,1)S(1)}, bf16[8...) custom-call(bf16[3,4,80,128]{3,2,1,0:T(8,128)(2,1)S(1)} %get-tuple-element.45.refs_0_, ...), custom_call_target="tpu_custom_call" | custom-call | tf_op jit(solution)/shard_map/weight_grads/pallas_call | solution.py:461
  14.0 0.1 collective-permute-start.3
  14.1 1.4 %collective-permute-start.4 = (bf16[224,128]{1,0:T(8,128)(2,1)S(1)}, bf16[224,128]{1,0:T(8,128)(2,1)S(1)}, u32[]{:S(2)}, u32[]{:S(2)}) collective-permute-start(bf16[224,128]{1,0:T(8,128)(2,1)S(1)} %get-tuple-element.60), channel_id=1, source_target_pairs={{0,2},{2,0},{1,3},{3,1},{4,6},{6,4},{5,7},{7,5},{8,10},{10,8},{9,1... | collective-permute-start | bytes 172040 | tf_op jit(solution)/shard_map/ppermute | solution.py:484
  15.4 0.0 collective-permute-done.6.refs_3_.refs_7_
  15.4 0.0 collective-permute-done.5.refs_2_.refs_6_
  15.4 0.9 %other_cells.1 = (bf16[4,6,80,128]{3,2,1,0:T(8,128)(2,1)S(1)}, bf16[4,6,80,128]{3,2,1,0:T(8,128)(2,1)S(1)}) custom-call(bf16[6,6,64,128]{3,2,1,0:T(8,128)(2,1)S(1)} %get-tuple-element.61.refs_0_, bf16[8,4,64,128]{3,2,1,0:T(8,128)(2,1)S(1)} %get-tuple-element.62.refs_1_, bf16[3,3,64,72]{3,2,1,0:T(8,128)(2,1)S(1)} %collective-permute-done.5.refs_2_.refs_6_, ...), custom_call_target="tpu_custom_call" | custom-call | flops 2147483648 | bytes 1048576 | tf_op jit(solution)/shard_map/other_cells/pallas_call | solution.py:486
  16.3 1.9 %collective-permute-done.3 = bf16[224,128]{1,0:T(8,128)(2,1)S(1)} collective-permute-done((bf16[224,128]{1,0:T(8,128)(2,1)S(1)}, bf16[224,128]{1,0:T(8,128)(2,1)S(1)}, u32[]{:S(2)}, u32[]{:S(2)}) %collective-permute-start.3) | collective-permute-done | bytes 57376 | tf_op jit(solution)/shard_map/ppermute | solution.py:483
  18.2 0.1 collective-permute-done.4
  18.4 1.8 %collective-permute-start.7 = (bf16[224,128]{1,0:T(8,128)(2,1)S(1)}, bf16[224,128]{1,0:T(8,128)(2,1)S(1)}, u32[]{:S(2)}, u32[]{:S(2)}) collective-permute-start(bf16[224,128]{1,0:T(8,128)(2,1)S(1)} %add.12), channel_id=1, source_target_pairs={{0,8},{4,12},{8,0},{12,4},{1,9},{5,13},{9,1},{13,5},{2,10},{6,14},... | collective-permute-start | bytes 172040 | tf_op jit(solution)/shard_map/ppermute | solution.py:499
  20.2 0.8 %collective-permute-start.8 = (bf16[224,128]{1,0:T(8,128)(2,1)S(1)}, bf16[224,128]{1,0:T(8,128)(2,1)S(1)}, u32[]{:S(2)}, u32[]{:S(2)}) collective-permute-start(bf16[224,128]{1,0:T(8,128)(2,1)S(1)} %add.13), channel_id=1, source_target_pairs={{0,4},{4,0},{8,12},{12,8},{1,5},{5,1},{9,13},{13,9},{2,6},{6,2},{1... | collective-permute-start | bytes 172040 | tf_op jit(solution)/shard_map/ppermute | solution.py:500
  21.0 1.6 %field_products.1 = (f32[6,4,32,128]{3,2,1,0:T(8,128)S(1)}, bf16[4,32,128]{2,1,0:T(8,128)(2,1)S(1)}, bf16[4,32,128]{2,1,0:T(8,128)(2,1)S(1)}, f32[6,4,32,128]{3,...) custom-call(bf16[4,6,80,128]{3,2,1,0:T(8,128)(2,1)S(1)} %get-tuple-element.57.refs_0_, ...), custom_call_target="tpu_custom_call" | custom-call | flops 2147483648 | bytes 1048576 | tf_op jit(solution)/shard_map/field_products/pallas_call | solution.py:504
  22.6 0.9 %collective-permute-done.7 = bf16[224,128]{1,0:T(8,128)(2,1)S(1)} collective-permute-done((bf16[224,128]{1,0:T(8,128)(2,1)S(1)}, bf16[224,128]{1,0:T(8,128)(2,1)S(1)}, u32[]{:S(2)}, u32[]{:S(2)}) %collective-permute-start.7) | collective-permute-done | bytes 57376 | tf_op jit(solution)/shard_map/ppermute | solution.py:499
  23.5 0.8 %collective-permute-done.8 = bf16[224,128]{1,0:T(8,128)(2,1)S(1)} collective-permute-done((bf16[224,128]{1,0:T(8,128)(2,1)S(1)}, bf16[224,128]{1,0:T(8,128)(2,1)S(1)}, u32[]{:S(2)}, u32[]{:S(2)}) %collective-permute-start.8) | collective-permute-done | bytes 57376 | tf_op jit(solution)/shard_map/ppermute | solution.py:500
  24.4 1.6 %collective-permute-start.9 = (bf16[416,128]{1,0:T(8,128)(2,1)S(1)}, bf16[416,128]{1,0:T(8,128)(2,1)S(1)}, u32[]{:S(2)}, u32[]{:S(2)}) collective-permute-start(bf16[416,128]{1,0:T(8,128)(2,1)S(1)} %pad_maximum_fusion.1), channel_id=1, source_target_pairs={{0,2},{2,0},{1,3},{3,1},{4,6},{6,4},{5,7},{7,5},{8,10},{10,8},{9,1... | collective-permute-start | bytes 319496 | tf_op jit(solution)/shard_map/ppermute | solution.py:534
  26.0 2.4 %collective-permute-start.10 = (bf16[352,128]{1,0:T(8,128)(2,1)S(1)}, bf16[352,128]{1,0:T(8,128)(2,1)S(1)}, u32[]{:S(2)}, u32[]{:S(2)}) collective-permute-start(bf16[352,128]{1,0:T(8,128)(2,1)S(1)} %pad_maximum_fusion.2), channel_id=1, source_target_pairs={{0,12},{4,8},{8,4},{12,0},{1,13},{5,9},{9,5},{13,1},{2,14},{6,10},... | collective-permute-start | bytes 270344 | tf_op jit(solution)/shard_map/ppermute | solution.py:533
  28.4 0.0 collective-permute-start.11
  28.4 4.3 %collective-permute-done.11.got_a = bf16[4,32,128]{2,1,0:T(8,128)(2,1)S(1)} collective-permute-done((bf16[4,32,128]{2,1,0:T(8,128)(2,1)S(1)}, bf16[4,32,128]{2,1,0:T(8,128)(2,1)S(1)}, u32[]{:S(2)}, u32[]{:S(2)}) %collective-permute-start.11) | collective-permute-done | bytes 32800 | tf_op jit(solution)/shard_map/ppermute | solution.py:535
  32.7 0.0 collective-permute-done.10.got_1
  32.7 0.0 collective-permute-done.9.got_0
  32.7 1.1 %last.1 = (bf16[6,4,32,128]{3,2,1,0:T(8,128)(2,1)}, bf16[6,4,32,128]{3,2,1,0:T(8,128)(2,1)}, f32[3,3,64,72]{3,2,1,0:T(8,128)}, f32[3,64,72]{2,1,0:T(8,128)}) custom-call(f32[6,4,32,128]{3,2,1,0:T(8,128)S(1)} %get-tuple-element.66.own, f32[6,4,32,128]{3,2,1,0:T(8,128)S(1)} %get-tuple-element.67.ig_own, bf16[224,128]{1,0:T(8,128)(2,1)S(1)} %add.14.half_0, ...), custom_call_target="tpu_custom_call" | custom-call | tf_op jit(solution)/shard_map/last/pallas_call | solution.py:536
  (7 shorter events, 0.1 us)
Async XLA Ops:
  0.6 7.7 %copy-start = (bf16[6,4,64,128]{3,2,1,0:T(8,128)(2,1)S(1)}, bf16[6,4,64,128]{3,2,1,0:T(8,128)(2,1)}, u32[]{:S(2)}) copy-start(bf16[6,4,64,128]{3,2,1,0:T(8,128)(2,1)} %x.1) | copy-start | bytes 1179652
  0.6 7.7 %copy-start.1 = (bf16[6,4,64,128]{3,2,1,0:T(8,128)(2,1)S(1)}, bf16[6,4,64,128]{3,2,1,0:T(8,128)(2,1)}, u32[]{:S(2)}) copy-start(bf16[6,4,64,128]{3,2,1,0:T(8,128)(2,1)} %u.1) | copy-start | bytes 1179652
  2.2 9.0 %collective-permute-start.1 = (bf16[4,64,128]{2,1,0:T(8,128)(2,1)}, bf16[4,64,128]{2,1,0:T(8,128)(2,1)S(1)}, u32[]{:S(2)}, u32[]{:S(2)}) collective-permute-start(bf16[4,64,128]{2,1,0:T(8,128)(2,1)} %get-tuple-element.48), channel_id=1, source_target_pairs={{0,13},{1,4},{4,1},{5,8},{8,5},{9,12},{12,9},{13,0},{2,15},{3,6},{... | collective-permute-start | bytes 196616 | tf_op jit(solution)/shard_map/ppermute | solution.py:425
  6.8 4.5 %collective-permute-start = (bf16[3,64,128]{2,1,0:T(8,128)(2,1)}, bf16[3,64,128]{2,1,0:T(8,128)(2,1)S(1)}, u32[]{:S(2)}, u32[]{:S(2)}) collective-permute-start(bf16[3,64,128]{2,1,0:T(8,128)(2,1)} %get-tuple-element.47), channel_id=1, source_target_pairs={{0,2},{2,0},{1,3},{3,1},{4,6},{6,4},{5,7},{7,5},{8,10},{10,8},{9,1... | collective-permute-start | bytes 147464 | tf_op jit(solution)/shard_map/ppermute | solution.py:427
  8.3 0.9 %copy-start.2 = (bf16[3,3,64,72]{3,2,1,0:T(8,128)(2,1)S(1)}, bf16[3,3,64,72]{3,2,1,0:T(8,128)(2,1)}, u32[]{:S(2)}) copy-start(bf16[3,3,64,72]{3,2,1,0:T(8,128)(2,1)} %refs_4_.1) | copy-start | bytes 248836
  9.2 0.8 %copy-start.3 = (bf16[3,72,64]{1,2,0:T(8,128)(2,1)S(1)}, bf16[3,72,64]{1,2,0:T(8,128)(2,1)}, u32[]{:S(2)}) copy-start(bf16[3,72,64]{1,2,0:T(8,128)(2,1)} %param.6) | copy-start | bytes 82948
  11.3 0.8 %copy-start.4 = (bf16[3,72,64]{1,2,0:T(8,128)(2,1)S(1)}, bf16[3,72,64]{1,2,0:T(8,128)(2,1)}, u32[]{:S(2)}) copy-start(bf16[3,72,64]{1,2,0:T(8,128)(2,1)} %param.6) | copy-start | bytes 82948
  11.3 1.4 %collective-permute-start.2 = (bf16[7,64,128]{2,1,0:T(8,128)(2,1)S(1)}, bf16[7,64,128]{2,1,0:T(8,128)(2,1)S(1)}, u32[]{:S(2)}, u32[]{:S(2)}) collective-permute-start(bf16[7,64,128]{2,1,0:T(8,128)(2,1)S(1)} %pad_maximum_fusion), channel_id=1, source_target_pairs={{0,1},{1,0},{2,3},{3,2},{4,5},{5,4},{6,7},{7,6},{8,9},{9,8},{10,11... | collective-permute-start | bytes 344072 | tf_op jit(solution)/shard_map/ppermute | solution.py:459
  11.4 4.1 %collective-permute-start.5 = (bf16[3,3,64,72]{3,2,1,0:T(8,128)(2,1)S(1)}, bf16[3,3,64,72]{3,2,1,0:T(8,128)(2,1)S(1)}, u32[]{:S(2)}, u32[]{:S(2)}) collective-permute-start(bf16[3,3,64,72]{3,2,1,0:T(8,128)(2,1)S(1)} %copy-done.2), channel_id=1, source_target_pairs={{0,1},{1,0},{2,3},{3,2},{4,5},{5,4},{6,7},{7,6},{8,9},{9,8},{10,11... | collective-permute-start | bytes 248840 | tf_op jit(solution)/shard_map/ppermute | solution.py:430
  12.1 3.4 %collective-permute-start.6 = (bf16[3,64,72]{2,1,0:T(8,128)(2,1)S(1)}, bf16[3,64,72]{2,1,0:T(8,128)(2,1)S(1)}, u32[]{:S(2)}, u32[]{:S(2)}) collective-permute-start(bf16[3,64,72]{2,1,0:T(8,128)(2,1)S(1)} %bitcast.7), channel_id=1, source_target_pairs={{0,1},{1,0},{2,3},{3,2},{4,5},{5,4},{6,7},{7,6},{8,9},{9,8},{10,11... | collective-permute-start | bytes 82952 | tf_op jit(solution)/shard_map/ppermute | solution.py:431
  14.0 4.2 %collective-permute-start.3 = (bf16[224,128]{1,0:T(8,128)(2,1)S(1)}, bf16[224,128]{1,0:T(8,128)(2,1)S(1)}, u32[]{:S(2)}, u32[]{:S(2)}) collective-permute-start(bf16[224,128]{1,0:T(8,128)(2,1)S(1)} %get-tuple-element.59), channel_id=1, source_target_pairs={{0,4},{4,0},{8,12},{12,8},{1,5},{5,1},{9,13},{13,9},{2,6},{6,2},{1... | collective-permute-start | bytes 172040 | tf_op jit(solution)/shard_map/ppermute | solution.py:483
  14.1 4.2 %collective-permute-start.4 = (bf16[224,128]{1,0:T(8,128)(2,1)S(1)}, bf16[224,128]{1,0:T(8,128)(2,1)S(1)}, u32[]{:S(2)}, u32[]{:S(2)}) collective-permute-start(bf16[224,128]{1,0:T(8,128)(2,1)S(1)} %get-tuple-element.60), channel_id=1, source_target_pairs={{0,2},{2,0},{1,3},{3,1},{4,6},{6,4},{5,7},{7,5},{8,10},{10,8},{9,1... | collective-permute-start | bytes 172040 | tf_op jit(solution)/shard_map/ppermute | solution.py:484
  18.4 5.1 %collective-permute-start.7 = (bf16[224,128]{1,0:T(8,128)(2,1)S(1)}, bf16[224,128]{1,0:T(8,128)(2,1)S(1)}, u32[]{:S(2)}, u32[]{:S(2)}) collective-permute-start(bf16[224,128]{1,0:T(8,128)(2,1)S(1)} %add.12), channel_id=1, source_target_pairs={{0,8},{4,12},{8,0},{12,4},{1,9},{5,13},{9,1},{13,5},{2,10},{6,14},... | collective-permute-start | bytes 172040 | tf_op jit(solution)/shard_map/ppermute | solution.py:499
  20.2 4.2 %collective-permute-start.8 = (bf16[224,128]{1,0:T(8,128)(2,1)S(1)}, bf16[224,128]{1,0:T(8,128)(2,1)S(1)}, u32[]{:S(2)}, u32[]{:S(2)}) collective-permute-start(bf16[224,128]{1,0:T(8,128)(2,1)S(1)} %add.13), channel_id=1, source_target_pairs={{0,4},{4,0},{8,12},{12,8},{1,5},{5,1},{9,13},{13,9},{2,6},{6,2},{1... | collective-permute-start | bytes 172040 | tf_op jit(solution)/shard_map/ppermute | solution.py:500
  24.4 8.3 %collective-permute-start.9 = (bf16[416,128]{1,0:T(8,128)(2,1)S(1)}, bf16[416,128]{1,0:T(8,128)(2,1)S(1)}, u32[]{:S(2)}, u32[]{:S(2)}) collective-permute-start(bf16[416,128]{1,0:T(8,128)(2,1)S(1)} %pad_maximum_fusion.1), channel_id=1, source_target_pairs={{0,2},{2,0},{1,3},{3,1},{4,6},{6,4},{5,7},{7,5},{8,10},{10,8},{9,1... | collective-permute-start | bytes 319496 | tf_op jit(solution)/shard_map/ppermute | solution.py:534
  26.0 6.7 %collective-permute-start.10 = (bf16[352,128]{1,0:T(8,128)(2,1)S(1)}, bf16[352,128]{1,0:T(8,128)(2,1)S(1)}, u32[]{:S(2)}, u32[]{:S(2)}) collective-permute-start(bf16[352,128]{1,0:T(8,128)(2,1)S(1)} %pad_maximum_fusion.2), channel_id=1, source_target_pairs={{0,12},{4,8},{8,4},{12,0},{1,13},{5,9},{9,5},{13,1},{2,14},{6,10},... | collective-permute-start | bytes 270344 | tf_op jit(solution)/shard_map/ppermute | solution.py:533
  28.4 4.3 %collective-permute-start.11 = (bf16[4,32,128]{2,1,0:T(8,128)(2,1)S(1)}, bf16[4,32,128]{2,1,0:T(8,128)(2,1)S(1)}, u32[]{:S(2)}, u32[]{:S(2)}) collective-permute-start(bf16[4,32,128]{2,1,0:T(8,128)(2,1)S(1)} %get-tuple-element.81), channel_id=1, source_target_pairs={{0,4},{4,0},{8,12},{12,8},{1,5},{5,1},{9,13},{13,9},{2,6},{6,2},{1... | collective-permute-start | bytes 98312 | tf_op jit(solution)/shard_map/ppermute | solution.py:535
